TPU v7x, 32 devices: a whole 2x2x4 slice. The times are simulated.
32 devices in a mesh: outer: 4 (over y, x), node: 8 (over z, core).
Axes of the slice: x: 2, y: 2, z: 4, core: 2. Of those that a mesh axis runs over, the one named last changes fastest.
Arguments:
- activations: bfloat16 [8192, 768], P(('outer', 'node')), may hold values from -6 to 6
- upstream: bfloat16 [8192, 4096], P(('outer', 'node')), may hold values from -0.13183594 to 0.13183594
- combine: float32 [8192], P(('outer', 'node')), may hold values from 0.05 to 1
- counts: int32 [32], P(('outer', 'node')), may hold values from 64 to 256, as said below
Outputs:
- weight_grad: float32 [768, 4096], P(('node', 'outer'))
Inputs may be any that keep to these rules, and one draw needn't show every extreme that they name: counts[i] is the number of filled slots of device i; slots at or after it are padding. Some device is full in every draw.
All inputs are finite; a program needn't handle non-finite values.
Results may differ from a plain program's by a relative error of at most 0.014.
Values may be sent and summed in bfloat16 or wider, within the bound.
A program may use at most 64 MiB of HBM per device.

v0:
```python
import jax
import jax.numpy as jnp
from jax import lax
from jax.sharding import PartitionSpec as P

BLOCK = 128


def body(activations, upstream, combine, counts):
    slots = activations.shape[0]
    width = upstream.shape[1]
    live = lax.iota(jnp.int32, slots) < counts[0]
    factor = jnp.where(live, combine, jnp.zeros_like(combine))
    scaled = (upstream.astype(jnp.float32) * factor[:, None]).astype(jnp.bfloat16)
    shard_rows = activations.shape[1] // lax.axis_size("node")
    partial_value = lax.dot_general(
        activations, scaled, (((0,), (0,)), ((), ())), preferred_element_type=jnp.float32
    )
    replica = lax.psum_scatter(
        partial_value.astype(jnp.bfloat16), "node", scatter_dimension=0, tiled=True
    ).astype(jnp.float32)
    blocks = replica.reshape(shard_rows, width // BLOCK, BLOCK)
    amax = jnp.max(jnp.abs(blocks), axis=2) + 1e-06
    scale_low = lax.optimization_barrier(amax.astype(jnp.bfloat16))
    quant = (blocks / scale_low.astype(jnp.float32)[..., None]).astype(jnp.bfloat16)
    quant = quant.reshape(shard_rows, width)
    got_quant, got_scale = (
        lax.all_to_all(quant, "outer", split_axis=0, concat_axis=0, tiled=True),
        lax.all_to_all(scale_low, "outer", split_axis=0, concat_axis=0, tiled=True),
    )
    sources = lax.axis_size("outer")
    owned = shard_rows // sources
    values = got_quant.astype(jnp.float32).reshape(sources, owned, width // BLOCK, BLOCK)
    scales = got_scale.astype(jnp.float32).reshape(sources, owned, width // BLOCK)
    restored = values * scales[..., None]
    return jnp.sum(restored, axis=0).reshape(owned, width)


def solution(mesh):
    return jax.shard_map(
        body,
        mesh=mesh,
        in_specs=(
            P(("outer", "node"), None),
            P(("outer", "node"), None),
            P(("outer", "node")),
            P(("outer", "node")),
        ),
        out_specs=P(("node", "outer"), None),
        check_vma=False,
    )
```

profile of v0, /device:TPU:0, one launch (start us, length us, event | category | flops | bytes accessed | tf_op | source)
XLA Modules:
  0.0 128.1 jit_solution(6008211163939779684)
XLA Ops:
  6.5 0.0 copy-start
  6.5 0.0 reduce-scatter.4.cloned.1.call-start
  7.2 0.7 compare_select_fusion
  7.9 0.0 copy-done
  7.9 6.4 %fusion = bf16[768,4096]{0,1:T(8,128)(2,1)} fusion(bf16[256,768]{1,0:T(8,128)(2,1)S(1)} %copy-done, bf16[256,4096]{1,0:T(8,128)(2,1)} %param.5, f32[256]{0:T(256)S(1)} %compare_select_fusion), kind=kOutput, calls=%fused_computation.1 | convolution fusion | flops 1616904192 | bytes 8782848 | tf_op jit(solution)/shard_map/dot_general | solution.py:16
  14.3 8.7 %copy.14 = bf16[768,4096]{1,0:T(8,128)(2,1)} copy(bf16[768,4096]{0,1:T(8,128)(2,1)} %fusion) | data formatting | bytes 12582912
  23.0 0.0 reduce-scatter.4.cloned.1.call-update
  23.1 72.7 %reduce-scatter.4.cloned.1.call-done = bf16[96,4096]{1,0:T(8,128)(2,1)} async-done(((bf16[768,4096]{1,0:T(8,128)(2,1)}), bf16[96,4096]{1,0:T(8,128)(2,1)}) %reduce-scatter.4.cloned.1.call-update) | async-done | bytes 786448 | tf_op jit(solution)/shard_map/reduce_scatter | solution.py:19
  95.7 1.3 %fusion.2 = f32[12,8,32,128]{3,1,2,0:T(8,128)S(1)} fusion(bf16[96,4096]{1,0:T(8,128)(2,1)} %reduce-scatter.4.cloned.1.call-done), kind=kLoop, calls=%fused_computation.6 | loop fusion | flops 786432 | bytes 2359296
  97.0 0.3 copy.16
  97.3 0.0 copy-start.1
  97.3 0.5 reduce_max.9
  97.8 0.7 reshape.21
  98.5 3.7 %all-to-all-start.1 = ((bf16[4,2,384]{2,1,0:T(2,128)(2,1)}), bf16[4,2,384]{2,1,0:T(2,128)(2,1)S(1)}, u32[]{:S(2)}, u32[]{:S(2)}) async-start(bf16[4,2,384]{2,1,0:T(2,128)(2,1)} %reshape.21), calls=%async_computation.1 | async-start | bytes 12288 | tf_op jit(solution)/shard_map/all_to_all | solution.py:29
  102.2 0.5 div.11
  102.6 0.0 copy-done.1
  102.7 1.9 %fusion.3 = bf16[96,4096]{1,0:T(8,128)(2,1)} fusion(bf16[96,4096]{1,0:T(8,128)(2,1)S(1)} %copy-done.1, f32[12,8,32,128]{3,2,1,0:T(8,128)S(1)} %bitcast.17), kind=kLoop, calls=%fused_computation.7 | loop fusion | flops 1179648 | bytes 3145728 | tf_op jit(solution)/shard_map/convert_element_type | solution.py:25
  104.5 2.4 %all-to-all-done.1 = bf16[4,2,384]{2,1,0:T(2,128)(2,1)S(1)} async-done(((bf16[4,2,384]{2,1,0:T(2,128)(2,1)}), bf16[4,2,384]{2,1,0:T(2,128)(2,1)S(1)}, u32[]{:S(2)}, u32[]{:S(2)}) %all-to-all-start.1) | async-done | bytes 6176 | tf_op jit(solution)/shard_map/all_to_all | solution.py:29
  106.9 4.2 %all-to-all-start = ((bf16[4,24,4096]{2,1,0:T(8,128)(2,1)}), bf16[4,24,4096]{2,1,0:T(8,128)(2,1)}, u32[]{:S(2)}, u32[]{:S(2)}) async-start(bf16[4,24,4096]{2,1,0:T(8,128)(2,1)} %bitcast.2), calls=%async_computation | async-start | bytes 1572864 | tf_op jit(solution)/shard_map/all_to_all | solution.py:28
  111.1 0.1 reshape.22
  111.1 0.5 mul.21
  111.6 0.3 mul.22
  111.9 7.2 %all-to-all-done = bf16[4,24,4096]{2,1,0:T(8,128)(2,1)} async-done(((bf16[4,24,4096]{2,1,0:T(8,128)(2,1)}), bf16[4,24,4096]{2,1,0:T(8,128)(2,1)}, u32[]{:S(2)}, u32[]{:S(2)}) %all-to-all-start) | async-done | bytes 786464 | tf_op jit(solution)/shard_map/all_to_all | solution.py:28
  119.1 2.1 %multiply_reduce_fusion = f32[24,4096]{1,0:T(8,128)} fusion(f32[4,24,4096]{2,1,0:T(8,128)S(1)} %mul.22, bf16[4,24,4096]{2,1,0:T(8,128)(2,1)} %all-to-all-done), kind=kLoop, calls=%fused_computation.8 | loop fusion | flops 1081344 | bytes 2752512 | tf_op jit(solution)/shard_map/reduce_sum | solution.py:36
  (1 shorter events, 0.0 us)
Async XLA Ops:
  6.5 1.4 %copy-start = (bf16[256,768]{1,0:T(8,128)(2,1)S(1)}, bf16[256,768]{1,0:T(8,128)(2,1)}, u32[]{:S(2)}) copy-start(bf16[256,768]{1,0:T(8,128)(2,1)} %param.4) | copy-start | bytes 1179652
  6.5 89.2 %reduce-scatter.4.cloned.1.call-start = ((), (), s32[]{:S(2)}) async-start(), calls=%async_computation.3 | async-start | bytes 7077888 | tf_op jit(solution)/shard_map/reduce_scatter | solution.py:19
  97.3 5.3 %copy-start.1 = (bf16[96,4096]{1,0:T(8,128)(2,1)S(1)}, bf16[96,4096]{1,0:T(8,128)(2,1)}, u32[]{:S(2)}) copy-start(bf16[96,4096]{1,0:T(8,128)(2,1)} %reduce-scatter.4.cloned.1.call-done) | copy-start | bytes 2359300
  98.5 8.3 %all-to-all-start.1 = ((bf16[4,2,384]{2,1,0:T(2,128)(2,1)}), bf16[4,2,384]{2,1,0:T(2,128)(2,1)S(1)}, u32[]{:S(2)}, u32[]{:S(2)}) async-start(bf16[4,2,384]{2,1,0:T(2,128)(2,1)} %reshape.21), calls=%async_computation.1 | async-start | bytes 12288 | tf_op jit(solution)/shard_map/all_to_all | solution.py:29
  106.9 12.3 %all-to-all-start = ((bf16[4,24,4096]{2,1,0:T(8,128)(2,1)}), bf16[4,24,4096]{2,1,0:T(8,128)(2,1)}, u32[]{:S(2)}, u32[]{:S(2)}) async-start(bf16[4,24,4096]{2,1,0:T(8,128)(2,1)} %bitcast.2), calls=%async_computation | async-start | bytes 1572864 | tf_op jit(solution)/shard_map/all_to_all | solution.py:28
Sparse Core Ops, SparseCore 0:
  23.2 72.5 reduce-scatter.3
where the time goes:
time: 129 us; the launch traced here: 128 us
  waiting for transfers between devices  82.3 us (64%)
  between operations  14.2 us (11%)
  local copies, waits for them, and re-layouts  11 us (9%)
  starting transfers between devices  7.84 us (6%)
  other arithmetic  6.4 us (5%)
  matrix products  6.37 us (5%)
    reduce_scatter x1, waiting for transfers between devices, body(): lax.psum_scatter(partial_value.astype(jnp.bfloat16), 'node', scatter_dime...  72.7 us
    unnamed x8, local copies, waits for them, and re-layouts  9.81 us
    all_to_all x1, waiting for transfers between devices, body(): lax.all_to_all(quant, 'outer', split_axis=0, concat_axis=0, tiled=True)  7.23 us
    dot_general x1, matrix products, body(): lax.dot_general(activations, scaled, (((0,), (0,)), ((), ())), preferred_...  6.37 us
    all_to_all x1, starting transfers between devices, body(): lax.all_to_all(quant, 'outer', split_axis=0, concat_axis=0, tiled=True)  4.19 us
    all_to_all x1, starting transfers between devices, body(): lax.all_to_all(scale_low, 'outer', split_axis=0, concat_axis=0, tiled=True)  3.65 us
  transfers between devices with their start and end apart: 3, of which 3 were waited for; matrix products, arithmetic and copies ran while one was open for 2% of the time, Pallas kernels for 0%

commit v1 on v0

--- a/solution.py
+++ b/solution.py
@@ -1,12 +1,19 @@
+import functools
 import jax
 import jax.numpy as jnp
 from jax import lax
+from jax.experimental import pallas as pl
+from jax.experimental.pallas import tpu as pltpu
 from jax.sharding import PartitionSpec as P
 
 BLOCK = 128
-
-
-def body(activations, upstream, combine, counts):
+CHUNK = 256
+HOP_LAG = 1
+SUM_LAG = 1
+MESH = pl.DeviceIdType.MESH
+
+
+def plain_body(activations, upstream, combine, counts):
     slots = activations.shape[0]
     width = upstream.shape[1]
     live = lax.iota(jnp.int32, slots) < counts[0]
@@ -36,7 +43,300 @@
     return jnp.sum(restored, axis=0).reshape(owned, width)
 
 
+def kernel(
+    n_outer, n_node, chunks, w,
+    acts_ref, up_ref, combine_ref, counts_ref, out_ref,
+    acts_t, mine, theirs, part, got, summed, back, to_peers, from_peers, to_owners,
+    a_send, a_recv, s_send, s_recv, z_send, z_recv, c_send, c_recv, d_send, d_recv,
+):
+    slots = acts_ref.shape[0]
+    line = n_node // 2
+    half = acts_t.shape[1] // 2
+    groups = n_node // 2
+    owned = out_ref.shape[0]
+    group_rows = owned * n_outer
+    cols = chunks * w
+    o = lax.axis_index("outer")
+    n = lax.axis_index("node")
+    c, k = n // 2, n % 2
+    sibling = c * 2 + (1 - k)
+    at_end = jnp.logical_or(c == 0, c == line - 1)
+    side = jnp.where(c == 0, 0, 1)
+
+    barrier = pltpu.get_barrier_semaphore()
+    for step in range(1, n_node):
+        pl.semaphore_signal(
+            barrier, inc=1, device_id=(o, lax.rem(n + step, n_node)), device_id_type=MESH
+        )
+    for step in range(1, n_outer):
+        pl.semaphore_signal(
+            barrier, inc=1, device_id=(lax.rem(o + step, n_outer), n), device_id_type=MESH
+        )
+
+    acts_t[0] = acts_ref[...].T
+    live = lax.broadcasted_iota(jnp.int32, (1, slots), 1) < counts_ref[0]
+    factor = jnp.where(live, combine_ref[...], 0.0)
+    factor = jnp.broadcast_to(factor, (BLOCK, slots)).T
+
+    def scaled(column):
+        parts = []
+        for b in range(w // BLOCK):
+            at = pl.ds(pl.multiple_of(column + b * BLOCK, BLOCK), BLOCK)
+            parts.append((up_ref[:, at].astype(jnp.float32) * factor).astype(jnp.bfloat16))
+        return jnp.concatenate(parts, axis=1) if len(parts) > 1 else parts[0]
+
+    @pl.loop(0, chunks)
+    def _(j):
+        theirs[j] = scaled((1 - k) * cols + j * w)
+
+    pl.semaphore_wait(barrier, n_node + n_outer - 2)
+
+    def acts_copy():
+        return pltpu.make_async_remote_copy(
+            src_ref=acts_t.at[0], dst_ref=acts_t.at[1], send_sem=a_send, recv_sem=a_recv,
+            device_id=(o, sibling), device_id_type=MESH,
+        )
+
+    def scaled_copy(j):
+        return pltpu.make_async_remote_copy(
+            src_ref=theirs.at[j], dst_ref=mine.at[1, j],
+            send_sem=s_send.at[j], recv_sem=s_recv.at[j],
+            device_id=(o, sibling), device_id_type=MESH,
+        )
+
+    def chain_copy(way, j, source):
+        onward = c - 1 if way == 0 else c + 1
+        return pltpu.make_async_remote_copy(
+            src_ref=source.at[way, j], dst_ref=got.at[way, j],
+            send_sem=z_send.at[way, j], recv_sem=z_recv.at[way, j],
+            device_id=(o, onward * 2 + k), device_id_type=MESH,
+        )
+
+    def peer_copy(j, to, slot):
+        return pltpu.make_async_remote_copy(
+            src_ref=to_peers.at[j, to], dst_ref=from_peers.at[j, slot],
+            send_sem=c_send.at[j, to], recv_sem=c_recv.at[j, slot],
+            device_id=(to, n), device_id_type=MESH,
+        )
+
+    def owner_copy(j, g, core, owner):
+        at = pl.ds(pl.multiple_of(core * cols + j * w, BLOCK), w)
+        return pltpu.make_async_remote_copy(
+            src_ref=to_owners.at[j, g], dst_ref=out_ref.at[:, at],
+            send_sem=d_send.at[j, g], recv_sem=d_recv.at[core, j],
+            device_id=(o, owner), device_id_type=MESH,
+        )
+
+    acts_copy().start()
+
+    @pl.loop(0, chunks)
+    def _(j):
+        scaled_copy(j).start()
+
+    @pl.loop(0, chunks)
+    def _(j):
+        mine[0, j] = scaled(k * cols + j * w)
+
+    acts_copy().wait_recv()
+
+    def chain_step(way, t):
+        lag = (line - 1 - c if way == 0 else c) * HOP_LAG
+        first = lag == 0
+        last = lag == (line - 1) * HOP_LAG
+        j = t - lag
+        inside = jnp.logical_and(j >= 0, j < chunks)
+
+        @pl.when(jnp.logical_and(inside, first))
+        def _():
+            chain_copy(way, j, part).start()
+
+        @pl.when(jnp.logical_and(inside, jnp.logical_not(jnp.logical_or(first, last))))
+        def _():
+            chain_copy(way, j, part).wait_recv()
+            summed[way, j] = (
+                got[way, j].astype(jnp.float32) + part[way, j].astype(jnp.float32)
+            ).astype(jnp.bfloat16)
+            chain_copy(way, j, summed).start()
+
+    def quantise_step(t):
+        j = t - (line - 1) * HOP_LAG
+
+        @pl.when(jnp.logical_and(at_end, jnp.logical_and(j >= 0, j < chunks)))
+        def _():
+            for way in range(2):
+
+                @pl.when(side == way)
+                def _(way=way):
+                    chain_copy(way, j, part).wait_recv()
+
+            for g in range(groups):
+                rows = pl.ds(g * group_rows, group_rows)
+                replica = got[side, j, rows, :].astype(jnp.float32) + part[
+                    side, j, rows, :
+                ].astype(jnp.float32)
+                for b in range(w // BLOCK):
+                    block = replica[:, b * BLOCK : (b + 1) * BLOCK]
+                    amax = jnp.max(jnp.abs(block), axis=1, keepdims=True) + 1e-06
+                    scale = amax.astype(jnp.bfloat16).astype(jnp.float32)
+                    quant = (block / scale).astype(jnp.bfloat16)
+                    back[rows, b * BLOCK : (b + 1) * BLOCK] = quant.astype(jnp.float32) * scale
+            for to in range(n_outer):
+                rows = [
+                    back[g * group_rows + to * owned : g * group_rows + (to + 1) * owned, :]
+                    for g in range(groups)
+                ]
+                rows = jnp.concatenate(rows, axis=0).astype(jnp.bfloat16)
+
+                @pl.when(o == to)
+                def _(rows=rows, to=to):
+                    from_peers[j, to] = rows
+
+                @pl.when(o != to)
+                def _(rows=rows, to=to):
+                    to_peers[j, to] = rows
+                    peer_copy(j, to, o).start()
+
+    def sum_step(t):
+        j = t - (line - 1) * HOP_LAG - SUM_LAG
+
+        @pl.when(jnp.logical_and(at_end, jnp.logical_and(j >= 0, j < chunks)))
+        def _():
+            for slot in range(n_outer):
+
+                @pl.when(o != slot)
+                def _(slot=slot):
+                    peer_copy(j, lax.rem(o + 1, n_outer), slot).wait_recv()
+
+            total = from_peers[j, 0].astype(jnp.float32)
+            for slot in range(1, n_outer):
+                total = total + from_peers[j, slot].astype(jnp.float32)
+            for g in range(groups):
+                owner = side * groups + g
+                rows = total[g * owned : (g + 1) * owned, :]
+
+                @pl.when(owner == n)
+                def _(rows=rows):
+                    at = pl.ds(pl.multiple_of(k * cols + j * w, BLOCK), w)
+                    out_ref[:, at] = rows
+
+                @pl.when(owner != n)
+                def _(rows=rows, g=g, owner=owner):
+                    to_owners[j, g] = rows
+                    owner_copy(j, g, k, owner).start()
+
+    @pl.loop(0, chunks + (line - 1) * HOP_LAG + SUM_LAG)
+    def _(t):
+        @pl.when(t < chunks)
+        def _():
+            scaled_copy(t).wait_recv()
+            value = jnp.dot(
+                acts_t[0], mine[0, t], preferred_element_type=jnp.float32
+            ) + jnp.dot(acts_t[1], mine[1, t], preferred_element_type=jnp.float32)
+            value = value.astype(jnp.bfloat16)
+            part[0, t] = value[:half]
+            part[1, t] = value[half:]
+
+        chain_step(0, t)
+        chain_step(1, t)
+        quantise_step(t)
+        sum_step(t)
+
+    end_chip = jnp.where(n < groups, 0, line - 1)
+
+    acts_copy().wait_send()
+
+    @pl.loop(0, chunks)
+    def _(j):
+        scaled_copy(j).wait_send()
+
+        @pl.when(c > 0)
+        def _():
+            chain_copy(0, j, part).wait_send()
+
+        @pl.when(c < line - 1)
+        def _():
+            chain_copy(1, j, part).wait_send()
+
+        @pl.when(at_end)
+        def _():
+            for to in range(n_outer):
+
+                @pl.when(o != to)
+                def _(to=to):
+                    peer_copy(j, to, o).wait_send()
+
+            for g in range(groups):
+
+                @pl.when(side * groups + g != n)
+                def _(g=g):
+                    owner_copy(j, g, k, sibling).wait_send()
+
+        for core in range(2):
+
+            @pl.when(end_chip * 2 + core != n)
+            def _(core=core):
+                owner_copy(j, 0, core, sibling).wait_recv()
+
+
+def fused_body(n_outer, n_node, activations, upstream, combine, counts):
+    slots, ffw = activations.shape
+    width = upstream.shape[1]
+    owned = ffw // (n_outer * n_node)
+    half, cols = ffw // 2, width // 2
+    w = CHUNK
+    chunks = cols // w
+    groups = n_node // 2
+    dma = pltpu.SemaphoreType.DMA
+    vmem = pltpu.VMEM
+    return pl.pallas_call(
+        functools.partial(kernel, n_outer, n_node, chunks, w),
+        out_shape=jax.ShapeDtypeStruct((owned, width), jnp.float32),
+        in_specs=[pl.BlockSpec(memory_space=pltpu.VMEM)] * 3
+        + [pl.BlockSpec(memory_space=pltpu.SMEM)],
+        out_specs=pl.BlockSpec(memory_space=pltpu.VMEM),
+        scratch_shapes=[
+            vmem((2, ffw, slots), jnp.bfloat16),
+            vmem((2, chunks, slots, w), jnp.bfloat16),
+            vmem((chunks, slots, w), jnp.bfloat16),
+            vmem((2, chunks, half, w), jnp.bfloat16),
+            vmem((2, chunks, half, w), jnp.bfloat16),
+            vmem((2, chunks, half, w), jnp.bfloat16),
+            vmem((half, w), jnp.float32),
+            vmem((chunks, n_outer, groups * owned, w), jnp.bfloat16),
+            vmem((chunks, n_outer, groups * owned, w), jnp.bfloat16),
+            vmem((chunks, groups, owned, w), jnp.float32),
+            dma, dma,
+            dma((chunks,)), dma((chunks,)),
+            dma((2, chunks)), dma((2, chunks)),
+            dma((chunks, n_outer)), dma((chunks, n_outer)),
+            dma((chunks, groups)), dma((2, chunks)),
+        ],
+        compiler_params=pltpu.CompilerParams(
+            collective_id=0, has_side_effects=True, vmem_limit_bytes=56 * 1024 * 1024
+        ),
+        cost_estimate=pl.CostEstimate(
+            flops=2 * slots * ffw * width, bytes_accessed=8 << 20, transcendentals=0
+        ),
+    )(activations, upstream, combine.reshape(1, slots), counts)
+
+
 def solution(mesh):
+    n_outer, n_node = mesh.shape["outer"], mesh.shape["node"]
+
+    def body(activations, upstream, combine, counts):
+        ffw, width = activations.shape[1], upstream.shape[1]
+        owned = ffw // (n_outer * n_node)
+        fits = (
+            n_node >= 4
+            and owned % 8 == 0
+            and (owned * n_outer) % 16 == 0
+            and (owned * n_node // 2) % 16 == 0
+            and (width // 2) % CHUNK == 0
+        )
+        if fits:
+            return fused_body(n_outer, n_node, activations, upstream, combine, counts)
+        return plain_body(activations, upstream, combine, counts)
+
     return jax.shard_map(
         body,
         mesh=mesh,

time: 129 us -> 70.5 us (0.55)
  waiting for transfers between devices: 82.3 us -> 0 us
  Pallas kernels: 0 us -> 67.9 us
  between operations: 14.2 us -> 0.66 us
  local copies, waits for them, and re-layouts: 11 us -> 1.77 us
  starting transfers between devices: 7.84 us -> 0 us
  other arithmetic: 6.4 us -> 0 us
  matrix products: 6.37 us -> 0 us
    reduce_scatter x1 -> x0, waiting for transfers between devices: 72.7 us -> none  [body(): lax.psum_scatter(partial_value.astype(jnp.bfloat16), 'node', scatter_dime...]
    pallas_call x0 -> x1, Pallas kernels: none -> 67.9 us  [fused_body(): pl.pallas_call(functools.partial(kernel, n_outer, n_node, chunks, w), out...]
    all_to_all x2 -> x0, waiting for transfers between devices: 9.59 us -> none  [the longest x1 7.23 us: body(): lax.all_to_all(quant, 'outer', split_axis=0, concat_axis=0, tiled=True)]
    unnamed x8 -> x1, local copies, waits for them, and re-layouts: 9.81 us -> 1.77 us
    all_to_all x2 -> x0, starting transfers between devices: 7.84 us -> none  [the longest x1 4.19 us: body(): lax.all_to_all(quant, 'outer', split_axis=0, concat_axis=0, tiled=True)]
    dot_general x1 -> x0, matrix products: 6.37 us -> none  [body(): lax.dot_general(activations, scaled, (((0,), (0,)), ((), ())), preferred_...]
    reduce_sum x1 -> x0, other arithmetic: 2.09 us -> none  [body(): return jnp.sum(restored, axis=0).reshape(owned, width)]
    convert_element_type x2 -> x0, other arithmetic: 1.86 us -> none  [the longest x1 1.85 us: body(): (blocks / scale_low.astype(jnp.float32)[..., None]).astype(jnp.bfloat16)]
  transfers between devices with their start and end apart: 3 -> 0, of which waited for: 3 -> 0; matrix products, arithmetic and copies ran while one was open for 2% -> 0% of each run, Pallas kernels for 0% -> 0%
where the time goes in v1:
time: 70.5 us; the launch traced here: 70.3 us
  Pallas kernels  67.9 us (96%)
  local copies, waits for them, and re-layouts  1.77 us (3%)
    pallas_call x1, Pallas kernels, fused_body(): pl.pallas_call(functools.partial(kernel, n_outer, n_node, chunks, w), out...  67.9 us
    unnamed x1, local copies, waits for them, and re-layouts  1.77 us

profile of v1, /device:TPU:0, one launch (start us, length us, event | category | flops | bytes accessed | tf_op | source)
XLA Modules:
  0.0 70.3 jit_solution(5342814413875000810)
XLA Ops:
  0.7 67.9 %shard_map.46 = f32[24,4096]{1,0:T(8,128)} custom-call(bf16[256,768]{1,0:T(8,128)(2,1)} %acts_ref.1, bf16[256,4096]{1,0:T(8,128)(2,1)} %up_ref.1, f32[1,256]{1,0:T(1,128)} %bitcast.1, s32[1]{0:T(128)S(6)} %copy.6.counts_ref), custom_call_target="tpu_custom_call" | custom-call | flops 1610612736 | bytes 8388608 | tf_op jit(solution)/shard_map/pallas_call | solution.py:291
  68.5 1.8 %copy.7 = f32[24,4096]{1,0:T(8,128)} copy(f32[24,4096]{1,0:T(8,128)} %shard_map.46) | data formatting | bytes 786432

commit v2 on v1

--- a/solution.py
+++ b/solution.py
@@ -7,9 +7,10 @@
 from jax.sharding import PartitionSpec as P
 
 BLOCK = 128
-CHUNK = 256
-HOP_LAG = 1
-SUM_LAG = 1
+CHUNK = 128
+PARTS = 1
+HOP_LAG = 2
+SUM_LAG = 3
 MESH = pl.DeviceIdType.MESH
 
 
@@ -46,13 +47,15 @@
 def kernel(
     n_outer, n_node, chunks, w,
     acts_ref, up_ref, combine_ref, counts_ref, out_ref,
-    acts_t, mine, theirs, part, got, summed, back, to_peers, from_peers, to_owners,
+    acts_t, mine, theirs, part, got, summed, back, to_peers, from_peers, stash, to_owners, from_ends,
     a_send, a_recv, s_send, s_recv, z_send, z_recv, c_send, c_recv, d_send, d_recv,
 ):
     slots = acts_ref.shape[0]
     line = n_node // 2
     half = acts_t.shape[1] // 2
     groups = n_node // 2
+    units = PARTS * chunks
+    part_groups = groups // PARTS
     owned = out_ref.shape[0]
     group_rows = owned * n_outer
     cols = chunks * w
@@ -119,11 +122,15 @@
             device_id=(to, n), device_id_type=MESH,
         )
 
-    def owner_copy(j, g, core, owner):
-        at = pl.ds(pl.multiple_of(core * cols + j * w, BLOCK), w)
-        return pltpu.make_async_remote_copy(
-            src_ref=to_owners.at[j, g], dst_ref=out_ref.at[:, at],
-            send_sem=d_send.at[j, g], recv_sem=d_recv.at[core, j],
+    def owner_of(unit, g):
+        p = unit // chunks
+        return side * groups + jnp.where(side == 0, PARTS - 1 - p, p) * part_groups + g
+
+    def owner_copy(pair, g, core, owner):
+        q = lax.rem(pair, chunks // 2)
+        return pltpu.make_async_remote_copy(
+            src_ref=to_owners.at[pair, g], dst_ref=from_ends.at[core, q],
+            send_sem=d_send.at[pair, g], recv_sem=d_recv.at[core, q],
             device_id=(o, owner), device_id_type=MESH,
         )
 
@@ -132,10 +139,6 @@
     @pl.loop(0, chunks)
     def _(j):
         scaled_copy(j).start()
-
-    @pl.loop(0, chunks)
-    def _(j):
-        mine[0, j] = scaled(k * cols + j * w)
 
     acts_copy().wait_recv()
 
@@ -144,7 +147,7 @@
         first = lag == 0
         last = lag == (line - 1) * HOP_LAG
         j = t - lag
-        inside = jnp.logical_and(j >= 0, j < chunks)
+        inside = jnp.logical_and(j >= 0, j < units)
 
         @pl.when(jnp.logical_and(inside, first))
         def _():
@@ -161,7 +164,7 @@
     def quantise_step(t):
         j = t - (line - 1) * HOP_LAG
 
-        @pl.when(jnp.logical_and(at_end, jnp.logical_and(j >= 0, j < chunks)))
+        @pl.when(jnp.logical_and(at_end, jnp.logical_and(j >= 0, j < units)))
         def _():
             for way in range(2):
 
@@ -169,7 +172,7 @@
                 def _(way=way):
                     chain_copy(way, j, part).wait_recv()
 
-            for g in range(groups):
+            for g in range(part_groups):
                 rows = pl.ds(g * group_rows, group_rows)
                 replica = got[side, j, rows, :].astype(jnp.float32) + part[
                     side, j, rows, :
@@ -183,7 +186,7 @@
             for to in range(n_outer):
                 rows = [
                     back[g * group_rows + to * owned : g * group_rows + (to + 1) * owned, :]
-                    for g in range(groups)
+                    for g in range(part_groups)
                 ]
                 rows = jnp.concatenate(rows, axis=0).astype(jnp.bfloat16)
 
@@ -199,7 +202,7 @@
     def sum_step(t):
         j = t - (line - 1) * HOP_LAG - SUM_LAG
 
-        @pl.when(jnp.logical_and(at_end, jnp.logical_and(j >= 0, j < chunks)))
+        @pl.when(jnp.logical_and(at_end, jnp.logical_and(j >= 0, j < units)))
         def _():
             for slot in range(n_outer):
 
@@ -210,31 +213,39 @@
             total = from_peers[j, 0].astype(jnp.float32)
             for slot in range(1, n_outer):
                 total = total + from_peers[j, slot].astype(jnp.float32)
-            for g in range(groups):
-                owner = side * groups + g
+            for g in range(part_groups):
+                owner = owner_of(j, g)
                 rows = total[g * owned : (g + 1) * owned, :]
 
                 @pl.when(owner == n)
                 def _(rows=rows):
-                    at = pl.ds(pl.multiple_of(k * cols + j * w, BLOCK), w)
+                    at = pl.ds(pl.multiple_of(k * cols + lax.rem(j, chunks) * w, BLOCK), w)
                     out_ref[:, at] = rows
 
                 @pl.when(owner != n)
-                def _(rows=rows, g=g, owner=owner):
-                    to_owners[j, g] = rows
-                    owner_copy(j, g, k, owner).start()
-
-    @pl.loop(0, chunks + (line - 1) * HOP_LAG + SUM_LAG)
+                def _(rows=rows, g=g):
+                    stash[g, pl.ds(pl.multiple_of(lax.rem(j, 2) * owned, 8), owned), :] = rows
+
+                @pl.when(jnp.logical_and(owner != n, lax.rem(j, 2) == 1))
+                def _(g=g, owner=owner):
+                    to_owners[j // 2, g] = stash[g].astype(jnp.bfloat16)
+                    owner_copy(j // 2, g, k, owner).start()
+
+    @pl.loop(0, units + (line - 1) * HOP_LAG + SUM_LAG)
     def _(t):
         @pl.when(t < chunks)
         def _():
+            mine[0, t] = scaled(k * cols + t * w)
             scaled_copy(t).wait_recv()
             value = jnp.dot(
                 acts_t[0], mine[0, t], preferred_element_type=jnp.float32
             ) + jnp.dot(acts_t[1], mine[1, t], preferred_element_type=jnp.float32)
             value = value.astype(jnp.bfloat16)
-            part[0, t] = value[:half]
-            part[1, t] = value[half:]
+            size = half // PARTS
+            for p in range(PARTS):
+                low = (PARTS - 1 - p) * size
+                part[0, p * chunks + t] = value[low : low + size]
+                part[1, p * chunks + t] = value[half + p * size : half + (p + 1) * size]
 
         chain_step(0, t)
         chain_step(1, t)
@@ -245,37 +256,45 @@
 
     acts_copy().wait_send()
 
+    @pl.loop(0, units)
+    def _(j):
+        @pl.when(c > 0)
+        def _():
+            chain_copy(0, j, part).wait_send()
+
+        @pl.when(c < line - 1)
+        def _():
+            chain_copy(1, j, part).wait_send()
+
+        @pl.when(at_end)
+        def _():
+            for to in range(n_outer):
+
+                @pl.when(o != to)
+                def _(to=to):
+                    peer_copy(j, to, o).wait_send()
+
+            for g in range(part_groups):
+
+                @pl.when(jnp.logical_and(owner_of(j, g) != n, lax.rem(j, 2) == 1))
+                def _(g=g):
+                    owner_copy(j // 2, g, k, sibling).wait_send()
+
     @pl.loop(0, chunks)
     def _(j):
         scaled_copy(j).wait_send()
 
-        @pl.when(c > 0)
-        def _():
-            chain_copy(0, j, part).wait_send()
-
-        @pl.when(c < line - 1)
-        def _():
-            chain_copy(1, j, part).wait_send()
-
-        @pl.when(at_end)
-        def _():
-            for to in range(n_outer):
-
-                @pl.when(o != to)
-                def _(to=to):
-                    peer_copy(j, to, o).wait_send()
-
-            for g in range(groups):
-
-                @pl.when(side * groups + g != n)
-                def _(g=g):
-                    owner_copy(j, g, k, sibling).wait_send()
-
+    @pl.loop(0, chunks // 2)
+    def _(q):
         for core in range(2):
 
             @pl.when(end_chip * 2 + core != n)
             def _(core=core):
-                owner_copy(j, 0, core, sibling).wait_recv()
+                owner_copy(q, 0, core, sibling).wait_recv()
+                both = from_ends[core, q].astype(jnp.float32)
+                for b in range(2):
+                    at = pl.ds(pl.multiple_of(core * cols + (2 * q + b) * w, BLOCK), w)
+                    out_ref[:, at] = both[b * owned : (b + 1) * owned]
 
 
 def fused_body(n_outer, n_node, activations, upstream, combine, counts):
@@ -285,7 +304,8 @@
     half, cols = ffw // 2, width // 2
     w = CHUNK
     chunks = cols // w
-    groups = n_node // 2
+    units = PARTS * chunks
+    part_groups = n_node // 2 // PARTS
     dma = pltpu.SemaphoreType.DMA
     vmem = pltpu.VMEM
     return pl.pallas_call(
@@ -298,18 +318,20 @@
             vmem((2, ffw, slots), jnp.bfloat16),
             vmem((2, chunks, slots, w), jnp.bfloat16),
             vmem((chunks, slots, w), jnp.bfloat16),
-            vmem((2, chunks, half, w), jnp.bfloat16),
-            vmem((2, chunks, half, w), jnp.bfloat16),
-            vmem((2, chunks, half, w), jnp.bfloat16),
-            vmem((half, w), jnp.float32),
-            vmem((chunks, n_outer, groups * owned, w), jnp.bfloat16),
-            vmem((chunks, n_outer, groups * owned, w), jnp.bfloat16),
-            vmem((chunks, groups, owned, w), jnp.float32),
+            vmem((2, units, half // PARTS, w), jnp.bfloat16),
+            vmem((2, units, half // PARTS, w), jnp.bfloat16),
+            vmem((2, units, half // PARTS, w), jnp.bfloat16),
+            vmem((half // PARTS, w), jnp.float32),
+            vmem((units, n_outer, part_groups * owned, w), jnp.bfloat16),
+            vmem((units, n_outer, part_groups * owned, w), jnp.bfloat16),
+            vmem((part_groups, 2 * owned, w), jnp.float32),
+            vmem((units // 2, part_groups, 2 * owned, w), jnp.bfloat16),
+            vmem((2, chunks // 2, 2 * owned, w), jnp.bfloat16),
             dma, dma,
             dma((chunks,)), dma((chunks,)),
-            dma((2, chunks)), dma((2, chunks)),
-            dma((chunks, n_outer)), dma((chunks, n_outer)),
-            dma((chunks, groups)), dma((2, chunks)),
+            dma((2, units)), dma((2, units)),
+            dma((units, n_outer)), dma((units, n_outer)),
+            dma((units // 2, part_groups)), dma((2, chunks // 2)),
         ],
         compiler_params=pltpu.CompilerParams(
             collective_id=0, has_side_effects=True, vmem_limit_bytes=56 * 1024 * 1024
@@ -330,8 +352,9 @@
             n_node >= 4
             and owned % 8 == 0
             and (owned * n_outer) % 16 == 0
-            and (owned * n_node // 2) % 16 == 0
-            and (width // 2) % CHUNK == 0
+            and n_node % (2 * PARTS) == 0
+            and (owned * n_node // (2 * PARTS)) % 16 == 0
+            and (width // 2) % (2 * CHUNK) == 0
         )
         if fits:
             return fused_body(n_outer, n_node, activations, upstream, combine, counts)

time: 70.5 us -> 64.9 us (0.921)
  Pallas kernels: 67.9 us -> 62.3 us
    pallas_call x1, Pallas kernels: 67.9 us -> 62.3 us  [fused_body(): pl.pallas_call(functools.partial(kernel, n_outer, n_node, chunks, w), out...]
where the time goes in v2:
time: 64.9 us; the launch traced here: 64.7 us
  Pallas kernels  62.3 us (96%)
  local copies, waits for them, and re-layouts  1.77 us (3%)
  between operations  0.66 us (1%)
    pallas_call x1, Pallas kernels, fused_body(): pl.pallas_call(functools.partial(kernel, n_outer, n_node, chunks, w), out...  62.3 us
    unnamed x1, local copies, waits for them, and re-layouts  1.77 us

profile of v2, /device:TPU:0, one launch (start us, length us, event | category | flops | bytes accessed | tf_op | source)
XLA Modules:
  0.0 64.7 jit_solution(5912268234339406673)
XLA Ops:
  0.7 62.3 %shard_map.46 = f32[24,4096]{1,0:T(8,128)} custom-call(bf16[256,768]{1,0:T(8,128)(2,1)} %acts_ref.1, bf16[256,4096]{1,0:T(8,128)(2,1)} %up_ref.1, f32[1,256]{1,0:T(1,128)} %bitcast.1, s32[1]{0:T(128)S(6)} %copy.6.counts_ref), custom_call_target="tpu_custom_call" | custom-call | flops 1610612736 | bytes 8388608 | tf_op jit(solution)/shard_map/pallas_call | solution.py:311
  62.9 1.8 %copy.7 = f32[24,4096]{1,0:T(8,128)} copy(f32[24,4096]{1,0:T(8,128)} %shard_map.46) | data formatting | bytes 786432

commit v3 on v2

--- a/solution.py
+++ b/solution.py
@@ -11,6 +11,7 @@
 PARTS = 1
 HOP_LAG = 2
 SUM_LAG = 3
+AHEAD = 2
 MESH = pl.DeviceIdType.MESH
 
 
@@ -88,56 +89,53 @@
             parts.append((up_ref[:, at].astype(jnp.float32) * factor).astype(jnp.bfloat16))
         return jnp.concatenate(parts, axis=1) if len(parts) > 1 else parts[0]
 
+    pl.semaphore_wait(barrier, n_node + n_outer - 2)
+
+    def acts_copy():
+        return pltpu.make_async_remote_copy(
+            src_ref=acts_t.at[0], dst_ref=acts_t.at[1], send_sem=a_send, recv_sem=a_recv,
+            device_id=(o, sibling), device_id_type=MESH,
+        )
+
+    def scaled_copy(j):
+        return pltpu.make_async_remote_copy(
+            src_ref=theirs.at[j], dst_ref=mine.at[1, j],
+            send_sem=s_send.at[j], recv_sem=s_recv.at[j],
+            device_id=(o, sibling), device_id_type=MESH,
+        )
+
+    def chain_copy(way, j, source):
+        onward = c - 1 if way == 0 else c + 1
+        return pltpu.make_async_remote_copy(
+            src_ref=source.at[way, j], dst_ref=got.at[way, j],
+            send_sem=z_send.at[way, j], recv_sem=z_recv.at[way, j],
+            device_id=(o, onward * 2 + k), device_id_type=MESH,
+        )
+
+    def peer_copy(j, to, slot):
+        return pltpu.make_async_remote_copy(
+            src_ref=to_peers.at[j, to], dst_ref=from_peers.at[j, slot],
+            send_sem=c_send.at[j, to], recv_sem=c_recv.at[j, slot],
+            device_id=(to, n), device_id_type=MESH,
+        )
+
+    def owner_of(unit, g):
+        p = unit // chunks
+        return side * groups + jnp.where(side == 0, PARTS - 1 - p, p) * part_groups + g
+
+    def owner_copy(pair, g, core, owner):
+        q = lax.rem(pair, chunks // 2)
+        return pltpu.make_async_remote_copy(
+            src_ref=to_owners.at[pair, g], dst_ref=from_ends.at[core, q],
+            send_sem=d_send.at[pair, g], recv_sem=d_recv.at[core, q],
+            device_id=(o, owner), device_id_type=MESH,
+        )
+
+    acts_copy().start()
+
     @pl.loop(0, chunks)
     def _(j):
         theirs[j] = scaled((1 - k) * cols + j * w)
-
-    pl.semaphore_wait(barrier, n_node + n_outer - 2)
-
-    def acts_copy():
-        return pltpu.make_async_remote_copy(
-            src_ref=acts_t.at[0], dst_ref=acts_t.at[1], send_sem=a_send, recv_sem=a_recv,
-            device_id=(o, sibling), device_id_type=MESH,
-        )
-
-    def scaled_copy(j):
-        return pltpu.make_async_remote_copy(
-            src_ref=theirs.at[j], dst_ref=mine.at[1, j],
-            send_sem=s_send.at[j], recv_sem=s_recv.at[j],
-            device_id=(o, sibling), device_id_type=MESH,
-        )
-
-    def chain_copy(way, j, source):
-        onward = c - 1 if way == 0 else c + 1
-        return pltpu.make_async_remote_copy(
-            src_ref=source.at[way, j], dst_ref=got.at[way, j],
-            send_sem=z_send.at[way, j], recv_sem=z_recv.at[way, j],
-            device_id=(o, onward * 2 + k), device_id_type=MESH,
-        )
-
-    def peer_copy(j, to, slot):
-        return pltpu.make_async_remote_copy(
-            src_ref=to_peers.at[j, to], dst_ref=from_peers.at[j, slot],
-            send_sem=c_send.at[j, to], recv_sem=c_recv.at[j, slot],
-            device_id=(to, n), device_id_type=MESH,
-        )
-
-    def owner_of(unit, g):
-        p = unit // chunks
-        return side * groups + jnp.where(side == 0, PARTS - 1 - p, p) * part_groups + g
-
-    def owner_copy(pair, g, core, owner):
-        q = lax.rem(pair, chunks // 2)
-        return pltpu.make_async_remote_copy(
-            src_ref=to_owners.at[pair, g], dst_ref=from_ends.at[core, q],
-            send_sem=d_send.at[pair, g], recv_sem=d_recv.at[core, q],
-            device_id=(o, owner), device_id_type=MESH,
-        )
-
-    acts_copy().start()
-
-    @pl.loop(0, chunks)
-    def _(j):
         scaled_copy(j).start()
 
     acts_copy().wait_recv()
@@ -148,10 +146,6 @@
         last = lag == (line - 1) * HOP_LAG
         j = t - lag
         inside = jnp.logical_and(j >= 0, j < units)
-
-        @pl.when(jnp.logical_and(inside, first))
-        def _():
-            chain_copy(way, j, part).start()
 
         @pl.when(jnp.logical_and(inside, jnp.logical_not(jnp.logical_or(first, last))))
         def _():
@@ -233,24 +227,34 @@
 
     @pl.loop(0, units + (line - 1) * HOP_LAG + SUM_LAG)
     def _(t):
-        @pl.when(t < chunks)
-        def _():
-            mine[0, t] = scaled(k * cols + t * w)
-            scaled_copy(t).wait_recv()
-            value = jnp.dot(
-                acts_t[0], mine[0, t], preferred_element_type=jnp.float32
-            ) + jnp.dot(acts_t[1], mine[1, t], preferred_element_type=jnp.float32)
-            value = value.astype(jnp.bfloat16)
-            size = half // PARTS
-            for p in range(PARTS):
-                low = (PARTS - 1 - p) * size
-                part[0, p * chunks + t] = value[low : low + size]
-                part[1, p * chunks + t] = value[half + p * size : half + (p + 1) * size]
+        @pl.when(t * AHEAD < chunks)
+        def _():
+            @pl.loop(t * AHEAD, t * AHEAD + AHEAD)
+            def _(t):
+                mine[0, t] = scaled(k * cols + t * w)
+                scaled_copy(t).wait_recv()
+                value = jnp.dot(
+                    acts_t[0], mine[0, t], preferred_element_type=jnp.float32
+                ) + jnp.dot(acts_t[1], mine[1, t], preferred_element_type=jnp.float32)
+                value = value.astype(jnp.bfloat16)
+                size = half // PARTS
+                for p in range(PARTS):
+                    low = (PARTS - 1 - p) * size
+                    part[0, p * chunks + t] = value[low : low + size]
+                    part[1, p * chunks + t] = value[half + p * size : half + (p + 1) * size]
+
+                @pl.when(c == line - 1)
+                def _():
+                    chain_copy(0, t, part).start()
+
+                @pl.when(c == 0)
+                def _():
+                    chain_copy(1, t, part).start()
 
         chain_step(0, t)
         chain_step(1, t)
+        sum_step(t)
         quantise_step(t)
-        sum_step(t)
 
     end_chip = jnp.where(n < groups, 0, line - 1)
 
@@ -355,6 +359,7 @@
             and n_node % (2 * PARTS) == 0
             and (owned * n_node // (2 * PARTS)) % 16 == 0
             and (width // 2) % (2 * CHUNK) == 0
+            and (width // 2 // CHUNK) % AHEAD == 0
         )
         if fits:
             return fused_body(n_outer, n_node, activations, upstream, combine, counts)

time: 64.9 us -> 63.6 us (0.980)
  Pallas kernels: 62.3 us -> 61 us
    pallas_call x1, Pallas kernels: 62.3 us -> 61 us  [fused_body(): pl.pallas_call(functools.partial(kernel, n_outer, n_node, chunks, w), out...]
where the time goes in v3:
time: 63.6 us; the launch traced here: 63.4 us
  Pallas kernels  61 us (96%)
  local copies, waits for them, and re-layouts  1.77 us (3%)
  between operations  0.66 us (1%)
    pallas_call x1, Pallas kernels, fused_body(): pl.pallas_call(functools.partial(kernel, n_outer, n_node, chunks, w), out...  61 us
    unnamed x1, local copies, waits for them, and re-layouts  1.77 us

profile of v3, /device:TPU:0, one launch (start us, length us, event | category | flops | bytes accessed | tf_op | source)
XLA Modules:
  0.0 63.4 jit_solution(11808380092594559622)
XLA Ops:
  0.7 61.0 %shard_map.46 = f32[24,4096]{1,0:T(8,128)} custom-call(bf16[256,768]{1,0:T(8,128)(2,1)} %acts_ref.1, bf16[256,4096]{1,0:T(8,128)(2,1)} %up_ref.1, f32[1,256]{1,0:T(1,128)} %bitcast.1, s32[1]{0:T(128)S(6)} %copy.6.counts_ref), custom_call_target="tpu_custom_call" | custom-call | flops 1610612736 | bytes 8388608 | tf_op jit(solution)/shard_map/pallas_call | solution.py:315
  61.7 1.8 %copy.7 = f32[24,4096]{1,0:T(8,128)} copy(f32[24,4096]{1,0:T(8,128)} %shard_map.46) | data formatting | bytes 786432
